TPU v7x, 32 devices: a whole 2x2x4 slice. The times are simulated.
32 devices in a mesh: grp: 4 (over x, core), dev: 8 (over z, y).
Axes of the slice: x: 2, y: 2, z: 4, core: 2. Of those that a mesh axis runs over, the one named last changes fastest.
Arguments:
- amplitudes: bfloat16 [32, 128, 128], P(('grp', 'dev')), may hold values from -2 to 2
- bases: bfloat16 [32, 256, 128], P(('grp', 'dev')), may hold values from -0.375 to 0.375
- factors: bfloat16 [32, 32, 256, 256], P(('grp', 'dev')), may hold values from -0.1875 to 0.1875
- intersections: bfloat16 [32, 4, 128, 128], P(('grp', 'dev')), may hold values from -0.25 to 0.25
- pair_integrals: float32 [32, 128, 128], P(('grp', 'dev')), may hold values from -6 to 6
- pno_energies: float32 [32, 128], P(('grp', 'dev')), may hold values from 0.3 to 3
- pair_shift: float32 [32], P(('grp', 'dev')), may hold values from 0.5 to 4
- pair_atoms: int32 [32, 2], P('grp'), may hold values from 0 to 7, all different within a row; in each aligned block of 8 rows (0 to 7, 8 to 15, ...) at most 3 rows name the same one
- pair_next: int32 [32, 4], P(('grp', 'dev')), may hold values from 0 to 15, as said below
Outputs:
- new_amplitudes: float32 [32, 128, 128], P(('grp', 'dev'))
Inputs may be any that keep to these rules, and one draw needn't show every extreme that they name: `pair_atoms`: each pair lists 2 different atoms of its own group. Within a group no atom is listed by more than 3 pairs, and some atom is listed by exactly 3 pairs of its group. `pair_next`: each pair lists 4 different pairs other than itself; a number below 8 is a pair of its own group, a number m from 8 on is pair m - 8 of the next group. Pairs of the last group list only pairs of their own group.
All inputs are finite; a program needn't handle non-finite values.
Results may differ from a plain program's by a relative error of at most 0.008.
Values may be sent and summed in bfloat16 or wider, within the bound.
No kernel may reach another device: no remote copies, remote signals or barrier semaphores. Data moves between devices by JAX's collectives and lax.ppermute only.
A program may use at most 128 MiB of HBM per device.

v0:
```python
import jax
import jax.numpy as jnp
from jax import lax
from jax.experimental import pallas as pl
from jax.experimental.pallas import tpu as pltpu
from jax.sharding import PartitionSpec as P

CAP = 3
ITERS = 2
F32 = jnp.float32
BF16 = jnp.bfloat16
CONTRACT_LAST = (((1,), (1,)), ((), ()))


def vmem_spec():
    return pl.BlockSpec(memory_space=pltpu.VMEM)


def smem_spec():
    return pl.BlockSpec(memory_space=pltpu.SMEM)


def params(mib):
    return pltpu.CompilerParams(vmem_limit_bytes=mib * 2**20)


def exchange(value, axis, offset):
    count = lax.axis_size(axis)
    return lax.ppermute(value, axis, [(d, d ^ offset) for d in range(count)])


def opposite(axis):
    return lax.axis_size(axis) // 2


def gather_across(value, axis):
    return jnp.concatenate([value, exchange(value, axis, opposite(axis))], axis=0)


def exchange_near(entries, axis):
    return [entries[0]] + [exchange(entries[j], axis, j) for j in range(1, len(entries))]


def gather_near(pair, axis):
    return exchange_near([pair] * (lax.axis_size(axis) // 2), axis)


def place_of(device, axis):
    half = lax.axis_size(axis) // 2
    offset = device ^ lax.axis_index(axis)
    return jnp.where(offset < half, offset, half + (offset ^ opposite(axis)))


def from_next(value, axis):
    count = lax.axis_size(axis)
    return lax.ppermute(value, axis, [(d, d - 1) for d in range(1, count)])


def stack_kernel(*refs):
    entries, out_ref = refs[:-1], refs[-1]
    for j, entry in enumerate(entries):
        for r in range(2):
            out_ref[r * len(entries) + j] = entry[r]


def stack(entries):
    _, rows, columns = entries[0].shape
    return pl.pallas_call(
        stack_kernel,
        in_specs=[vmem_spec()] * len(entries),
        out_specs=vmem_spec(),
        out_shape=jax.ShapeDtypeStruct((2 * len(entries), rows, columns), entries[0].dtype),
        compiler_params=params(16),
        name="stack",
    )(*entries)


def project_kernel(given, slots, *refs):
    base_refs, (factors_ref, out_ref, wide, narrow, half) = refs[:given], refs[given:]
    aux, npno = factors_ref.shape[0], narrow.shape[2]

    @pl.when(pl.program_id(0) == 0)
    def _():
        for s in range(CAP):
            for j in range(given):

                @pl.when(lax.rem(slots[s], given) == j)
                def _():
                    narrow[s] = base_refs[j][slots[s] // given]

            wide[pl.ds(s * npno, npno), :] = narrow[s].astype(F32).T.astype(BF16)

    for k in range(aux):
        left = jnp.dot(wide[...], factors_ref[k], preferred_element_type=F32).astype(BF16)
        for s in range(CAP):
            half[s, pl.ds(k * npno, npno), :] = left[s * npno : (s + 1) * npno]
    for s in range(CAP):
        both = jnp.dot(half[s], narrow[s], preferred_element_type=F32).astype(BF16)
        for k in range(aux):
            out_ref[s, k // 2, :, pl.ds((k % 2) * npno, npno)] = both[k * npno : (k + 1) * npno]


def project(slots, group_bases, factor_block, step=8):
    aux, width, _ = factor_block.shape
    given = len(group_bases)
    npno = group_bases[0].shape[2]
    step = min(step, aux)

    def kernel(*refs):
        project_kernel(given, *refs)

    return pl.pallas_call(
        kernel,
        grid=(aux // step,),
        in_specs=[smem_spec()]
        + [pl.BlockSpec((2, width, npno), lambda i: (0, 0, 0))] * given
        + [pl.BlockSpec((step, width, width), lambda i: (i, 0, 0))],
        out_specs=pl.BlockSpec((CAP, step // 2, npno, 2 * npno), lambda i: (0, i, 0, 0)),
        out_shape=jax.ShapeDtypeStruct((CAP, aux // 2, npno, 2 * npno), BF16),
        scratch_shapes=[
            pltpu.VMEM((CAP * npno, width), BF16),
            pltpu.VMEM((CAP, width, npno), BF16),
            pltpu.VMEM((CAP, step * npno, width), BF16),
        ],
        compiler_params=params(48),
        cost_estimate=pl.CostEstimate(
            flops=4 * CAP * aux * npno * width * (width + npno) // 2,
            bytes_accessed=2 * aux * width * width,
            transcendentals=0,
        ),
        name="project",
    )(slots, *group_bases, factor_block)


def ladder_kernel(given, slots, pairs, *refs):
    amp_refs, proj_ref, out_refs = refs[:given], refs[given], refs[given + 1 : 2 * given + 1]
    twice, mixed = refs[2 * given + 1 :]
    half, npno = proj_ref.shape[1], proj_ref.shape[2]
    s = pl.program_id(0)

    @pl.when(s == 0)
    def _():
        twice[...] = jnp.zeros_like(twice)
        for out_ref in out_refs:
            out_ref[...] = jnp.zeros_like(out_ref)

    for j in range(given):

        @pl.when(lax.rem(slots[s], given) == j)
        def _():
            amp = amp_refs[j][slots[s] // given]
            twice[pl.ds(0, npno), pl.ds(0, npno)] = amp
            twice[pl.ds(npno, npno), pl.ds(npno, npno)] = amp

    flat = proj_ref[0].reshape(half * npno, 2 * npno)
    mixed[...] = jnp.dot(flat, twice[...], preferred_element_type=F32).astype(BF16)
    total = jnp.zeros((npno, npno), F32)
    for m in range(half):
        total = total + lax.dot_general(
            mixed[pl.ds(m * npno, npno), :],
            proj_ref[0, m],
            CONTRACT_LAST,
            preferred_element_type=F32,
        )
    narrow = total.astype(BF16)
    for j in range(given):

        @pl.when((pairs[s] >= 0) & (lax.rem(slots[s], given) == j))
        def _():
            out_refs[j][slots[s] // given] = narrow


def ladder(slots, pairs, group_amps, projected):
    given = len(group_amps)
    half, npno = projected.shape[1:3]

    def kernel(*refs):
        ladder_kernel(given, *refs)

    return pl.pallas_call(
        kernel,
        grid=(CAP,),
        in_specs=[smem_spec()] * 2
        + [vmem_spec()] * given
        + [pl.BlockSpec((1, half, npno, 2 * npno), lambda s: (s, 0, 0, 0))],
        out_specs=[vmem_spec()] * given,
        out_shape=[jax.ShapeDtypeStruct((2, npno, npno), BF16)] * given,
        scratch_shapes=[
            pltpu.VMEM((2 * npno, 2 * npno), BF16),
            pltpu.VMEM((half * npno, 2 * npno), BF16),
        ],
        compiler_params=params(24),
        cost_estimate=pl.CostEstimate(
            flops=0,
            bytes_accessed=16 * CAP * half * npno**2,
            transcendentals=0,
        ),
        name="ladder",
    )(slots, pairs, *group_amps, projected)


def coupling_kernel(near, own_ref, next_ref, inter_ref, ints_ref, out_ref):
    count = own_ref.shape[0]
    total = ints_ref[...]
    for n in range(inter_ref.shape[0]):
        at = near[n]
        own = own_ref[jnp.minimum(at, count - 1)]
        far = next_ref[jnp.maximum(at - count, 0)]
        amp = jnp.where(at < count, own, far)
        inter = inter_ref[n]
        mixed = jnp.dot(inter, amp, preferred_element_type=F32).astype(BF16)
        total = total + lax.dot_general(
            mixed, inter, CONTRACT_LAST, preferred_element_type=F32
        )
    out_ref[...] = total


def coupling(near, own, following, inter, ints):
    return pl.pallas_call(
        coupling_kernel,
        in_specs=[smem_spec()] + [pl.BlockSpec()] * 4,
        out_specs=vmem_spec(),
        out_shape=jax.ShapeDtypeStruct(ints.shape, F32),
        compiler_params=params(16),
        name="coupling",
    )(near, own, following, inter, ints)


def fold_kernel(given, last, *refs):
    term_refs, (rest, down, across, far_down, far_across), (send, keep) = (
        refs[:given],
        refs[given : given + 5],
        refs[given + 5 :],
    )
    mine, other = (sum(ref[r].astype(F32) for ref in term_refs) for r in range(2))
    mine = mine + rest[...]
    keep[0] = mine
    if last:
        send[0] = other.astype(BF16)
    else:
        send[0] = other.astype(BF16)
        send[1] = (-mine / (down[...] + across[...])).astype(BF16)
        keep[1] = -other / (far_down[...] + far_across[...])


def fold(last, terms, rest, energies):
    given = len(terms)
    rows = 1 if last else 2

    def kernel(*refs):
        fold_kernel(given, last, *refs)

    return pl.pallas_call(
        kernel,
        in_specs=[vmem_spec()] * (given + 5),
        out_specs=[vmem_spec()] * 2,
        out_shape=[
            jax.ShapeDtypeStruct((rows,) + rest.shape, BF16),
            jax.ShapeDtypeStruct((rows,) + rest.shape, F32),
        ],
        compiler_params=params(16),
        name="fold",
    )(*terms, rest, *energies)


def finish_kernel(last, keep, got, down, across, out_ref):
    update = -(keep[0] + got[0].astype(F32)) / (down[...] + across[...])
    out_ref[0] = update.astype(out_ref.dtype)
    if not last:
        out_ref[1] = (keep[1] + got[1].astype(F32)).astype(out_ref.dtype)


def finish(last, keep, got, down, across):
    def kernel(*refs):
        finish_kernel(last, *refs)

    return pl.pallas_call(
        kernel,
        in_specs=[vmem_spec()] * 4,
        out_specs=vmem_spec(),
        out_shape=jax.ShapeDtypeStruct(keep.shape, F32 if last else BF16),
        compiler_params=params(16),
        name="finish",
    )(keep, got, down, across)


def on_device(
    amplitudes,
    bases,
    factors,
    intersections,
    pair_integrals,
    pno_energies,
    pair_shift,
    pair_atoms,
    pair_next,
):
    me = lax.axis_index("dev")
    count = lax.axis_size("dev")
    places = jnp.arange(count, dtype=jnp.int32)
    listed = jnp.any(pair_atoms == me, axis=1)
    before = places[None, :] < places[:, None]
    rank = jnp.sum(before & listed[None, :], axis=1)
    chosen = listed[None, :] & (rank[None, :] == jnp.arange(CAP)[:, None])
    pairs = jnp.sum(jnp.where(chosen, places[None, :] + 1, 0), axis=1) - 1
    slots = jnp.where(pairs >= 0, place_of(pairs, "dev"), 0)
    near = pair_next[0]
    near = jnp.where(
        near < count, place_of(near, "dev"), count + place_of(near - count, "dev")
    )
    inter = intersections[0]
    ints = pair_integrals[0]

    far_amps = exchange(amplitudes, "dev", opposite("dev"))
    pair_bases = gather_across(bases, "dev")
    shifted = pno_energies + 0.5 * pair_shift[:, None]
    far_shifted = exchange(shifted, "dev", opposite("dev"))
    amps, far_amps, far_shifted, pair_bases = lax.optimization_barrier(
        (amplitudes, far_amps, far_shifted, pair_bases)
    )
    group_bases = gather_near(pair_bases, "dev")
    group_amps = gather_near(jnp.concatenate([amps, far_amps], axis=0), "dev")
    energies = (shifted.reshape(-1, 1), shifted, far_shifted.reshape(-1, 1), far_shifted)
    projected = project(slots, group_bases, factors[0])
    group_amps, projected = lax.optimization_barrier((group_amps, projected))
    for iteration in range(ITERS):
        last = iteration + 1 == ITERS
        stacked = stack(group_amps)
        group_amps, stacked = lax.optimization_barrier((group_amps, stacked))
        following = from_next(stacked, "grp")
        terms = ladder(slots, pairs, group_amps, projected)
        rest = coupling(near, stacked, following, inter, ints)
        send, keep = fold(last, exchange_near(terms, "dev"), rest, energies)
        update = finish(last, keep, exchange(send, "dev", opposite("dev")), *energies[:2])
        if not last:
            group_amps = gather_near(update, "dev")
    return update


def solution(mesh):
    return jax.shard_map(
        on_device,
        mesh=mesh,
        in_specs=(
            P(("grp", "dev"), None, None),
            P(("grp", "dev"), None, None),
            P(("grp", "dev"), None, None, None),
            P(("grp", "dev"), None, None, None),
            P(("grp", "dev"), None, None),
            P(("grp", "dev"), None),
            P(("grp", "dev")),
            P("grp", None),
            P(("grp", "dev"), None),
        ),
        out_specs=P(("grp", "dev"), None, None),
        check_vma=False,
    )
```

profile of v0, /device:TPU:0, one launch (start us, length us, event | category | flops | bytes accessed | tf_op | source)
XLA Modules:
  0.0 77.0 jit_solution(4556675252822727795)
XLA Ops:
  0.0 4.0 %collective-permute-start = (bf16[1,128,128]{2,1,0:T(8,128)(2,1)}, bf16[1,128,128]{2,1,0:T(8,128)(2,1)S(1)}, u32[]{:S(2)}, u32[]{:S(2)}) collective-permute-start(bf16[1,128,128]{2,1,0:T(8,128)(2,1)} %param.9), channel_id=1, source_target_pairs={{0,4},{1,5},{2,6},{3,7},{4,0},{5,1},{6,2},{7,3},{8,12},{9,13},{10,... | collective-permute-start | bytes 98312 | tf_op jit(solution)/shard_map/ppermute | solution.py:29
  5.4 2.9 %collective-permute-start.2 = (bf16[1,256,128]{2,1,0:T(8,128)(2,1)}, bf16[1,256,128]{2,1,0:T(8,128)(2,1)S(1)}, u32[]{:S(2)}, u32[]{:S(2)}) collective-permute-start(bf16[1,256,128]{2,1,0:T(8,128)(2,1)} %param.10), channel_id=1, source_target_pairs={{0,4},{1,5},{2,6},{3,7},{4,0},{5,1},{6,2},{7,3},{8,12},{9,13},{10,... | collective-permute-start | bytes 196616 | tf_op jit(solution)/shard_map/ppermute | solution.py:29
  9.2 1.9 %collective-permute-done.2 = bf16[1,256,128]{2,1,0:T(8,128)(2,1)S(1)} collective-permute-done((bf16[1,256,128]{2,1,0:T(8,128)(2,1)}, bf16[1,256,128]{2,1,0:T(8,128)(2,1)S(1)}, u32[]{:S(2)}, u32[]{:S(2)}) %collective-permute-start.2) | collective-permute-done | bytes 65568 | tf_op jit(solution)/shard_map/ppermute | solution.py:29
  11.1 0.9 %pad_maximum_fusion.refs_1_ = bf16[2,256,128]{2,1,0:T(8,128)(2,1)S(1)} fusion(bf16[1,256,128]{2,1,0:T(8,128)(2,1)S(1)} %collective-permute-done.2, bf16[1,256,128]{2,1,0:T(8,128)(2,1)} %param.10), kind=kLoop, calls=%fused_computation | loop fusion | flops 65536 | bytes 262144 | tf_op jit(solution)/shard_map/concatenate | solution.py:37
  12.0 1.6 %collective-permute-start.6 = (bf16[2,256,128]{2,1,0:T(8,128)(2,1)S(1)}, bf16[2,256,128]{2,1,0:T(8,128)(2,1)S(1)}, u32[]{:S(2)}, u32[]{:S(2)}) collective-permute-start(bf16[2,256,128]{2,1,0:T(8,128)(2,1)S(1)} %pad_maximum_fusion.refs_1_), channel_id=1, source_target_pairs={{0,1},{1,0},{2,3},{3,2},{4,5},{5,4},{6,7},{7,6},{8,9},{9,8},{10,11... | collective-permute-start | bytes 393224 | tf_op jit(solution)/shard_map/ppermute | solution.py:29
  13.6 1.5 %collective-permute-start.7 = (bf16[2,256,128]{2,1,0:T(8,128)(2,1)S(1)}, bf16[2,256,128]{2,1,0:T(8,128)(2,1)S(1)}, u32[]{:S(2)}, u32[]{:S(2)}) collective-permute-start(bf16[2,256,128]{2,1,0:T(8,128)(2,1)S(1)} %pad_maximum_fusion.refs_1_), channel_id=1, source_target_pairs={{0,2},{1,3},{2,0},{3,1},{4,6},{5,7},{6,4},{7,5},{8,10},{9,11},{10,... | collective-permute-start | bytes 393224 | tf_op jit(solution)/shard_map/ppermute | solution.py:29
  16.3 1.6 %collective-permute-start.3 = (bf16[2,128,128]{2,1,0:T(8,128)(2,1)S(1)}, bf16[2,128,128]{2,1,0:T(8,128)(2,1)S(1)}, u32[]{:S(2)}, u32[]{:S(2)}) collective-permute-start(bf16[2,128,128]{2,1,0:T(8,128)(2,1)S(1)} %constant_dynamic-update-slice_fusion.refs_0_.refs_2_), channel_id=1, source_target_pairs={{0,1},{1,0},{2,3},{3,2},{4,5},{5,4},{6,7},{7,6},{8,9},{9,8},{10,11... | collective-permute-start | bytes 196616 | tf_op jit(solution)/shard_map/ppermute | solution.py:29
  17.9 1.5 %collective-permute-start.4 = (bf16[2,128,128]{2,1,0:T(8,128)(2,1)S(1)}, bf16[2,128,128]{2,1,0:T(8,128)(2,1)S(1)}, u32[]{:S(2)}, u32[]{:S(2)}) collective-permute-start(bf16[2,128,128]{2,1,0:T(8,128)(2,1)S(1)} %constant_dynamic-update-slice_fusion.refs_0_.refs_2_), channel_id=1, source_target_pairs={{0,2},{1,3},{2,0},{3,1},{4,6},{5,7},{6,4},{7,5},{8,10},{9,11},{10,... | collective-permute-start | bytes 196616 | tf_op jit(solution)/shard_map/ppermute | solution.py:29
  19.4 2.2 %collective-permute-start.5 = (bf16[2,128,128]{2,1,0:T(8,128)(2,1)S(1)}, bf16[2,128,128]{2,1,0:T(8,128)(2,1)S(1)}, u32[]{:S(2)}, u32[]{:S(2)}) collective-permute-start(bf16[2,128,128]{2,1,0:T(8,128)(2,1)S(1)} %constant_dynamic-update-slice_fusion.refs_0_.refs_2_), channel_id=1, source_target_pairs={{0,3},{1,2},{2,1},{3,0},{4,7},{5,6},{6,5},{7,4},{8,11},{9,10},{10,... | collective-permute-start | bytes 196616 | tf_op jit(solution)/shard_map/ppermute | solution.py:29
  22.1 6.1 %project.1.refs_6_ = bf16[3,16,128,256]{3,2,1,0:T(8,128)(2,1)S(1)} custom-call(s32[3]{0:T(128)S(1)} %get-tuple-element.68.refs_0_, bf16[2,256,128]{2,1,0:T(8,128)(2,1)S(1)} %pad_maximum_fusion.refs_1_, bf16[2,256,128]{2,1,0:T(8,128)(2,1)S(1)} %collective-permute-done.6.refs_2_, bf16[2,256,128]{2,1,0:T(8,128)(2,1)S(1)} %collective-permute-done.7.refs_3_, ...), custom_call_target="tpu_custom_call" | custom-call | flops 2415919104 | bytes 4194304 | tf_op jit(solution)/shard_map/project/pallas_call | solution.py:112
  28.3 1.3 %collective-permute-start.12 = (bf16[8,128,128]{2,1,0:T(8,128)(2,1)S(1)}, bf16[8,128,128]{2,1,0:T(8,128)(2,1)}, u32[]{:S(2)}, u32[]{:S(2)}) collective-permute-start(bf16[8,128,128]{2,1,0:T(8,128)(2,1)S(1)} %stack.2.own_ref), channel_id=1, source_target_pairs={{8,0},{16,8},{24,16},{9,1},{17,9},{25,17},{10,2},{18,10},{26,18},{... | collective-permute-start | bytes 786440 | tf_op jit(solution)/shard_map/ppermute | solution.py:56
  29.6 4.1 %ladder.2 = (bf16[2,128,128]{2,1,0:T(8,128)(2,1)S(1)}, bf16[2,128,128]{2,1,0:T(8,128)(2,1)}, bf16[2,128,128]{2,1,0:T(8,128)(2,1)}, bf16[2,128,128]{2,1,0:T(8,128)(2,1)}) custom-call(s32[3]{0:T(128)S(1)} %get-tuple-element.68.refs_0_, s32[3]{0:T(128)S(1)} %get-tuple-element.67.refs_1_, ...), custom_call_target="tpu_custom_call" | custom-call | bytes 12582912 | tf_op jit(solution)/shard_map/ladder/pallas_call | solution.py:180
  35.2 1.5 %collective-permute-start.10 = (bf16[2,128,128]{2,1,0:T(8,128)(2,1)}, bf16[2,128,128]{2,1,0:T(8,128)(2,1)}, u32[]{:S(2)}, u32[]{:S(2)}) collective-permute-start(bf16[2,128,128]{2,1,0:T(8,128)(2,1)} %get-tuple-element.50), channel_id=1, source_target_pairs={{0,2},{1,3},{2,0},{3,1},{4,6},{5,7},{6,4},{7,5},{8,10},{9,11},{10,... | collective-permute-start | bytes 196616 | tf_op jit(solution)/shard_map/ppermute | solution.py:29
  36.7 1.1 %collective-permute-start.11 = (bf16[2,128,128]{2,1,0:T(8,128)(2,1)}, bf16[2,128,128]{2,1,0:T(8,128)(2,1)}, u32[]{:S(2)}, u32[]{:S(2)}) collective-permute-start(bf16[2,128,128]{2,1,0:T(8,128)(2,1)} %get-tuple-element.51), channel_id=1, source_target_pairs={{0,3},{1,2},{2,1},{3,0},{4,7},{5,6},{6,5},{7,4},{8,11},{9,10},{10,... | collective-permute-start | bytes 196616 | tf_op jit(solution)/shard_map/ppermute | solution.py:29
  38.7 0.9 %copy-done = bf16[1,4,128,128]{3,2,1,0:T(8,128)(2,1)S(1)} copy-done((bf16[1,4,128,128]{3,2,1,0:T(8,128)(2,1)S(1)}, bf16[1,4,128,128]{3,2,1,0:T(8,128)(2,1)}, u32[]{:S(2)}) %copy-start) | copy-done | bytes 131096
  39.6 0.8 %copy-done.2 = f32[1,128,128]{2,1,0:T(8,128)S(1)} copy-done((f32[1,128,128]{2,1,0:T(8,128)S(1)}, f32[1,128,128]{2,1,0:T(8,128)}, u32[]{:S(2)}) %copy-start.2) | copy-done | bytes 65560
  41.1 1.5 %coupling.2.refs_4_ = f32[128,128]{1,0:T(8,128)S(1)} custom-call(s32[4]{0:T(128)S(1)} %copy-done.6, bf16[8,128,128]{2,1,0:T(8,128)(2,1)S(1)} %stack.2.own_ref, bf16[8,128,128]{2,1,0:T(8,128)(2,1)} %collective-permute-done.12.next_ref, bf16[4,128,128]{2,1,0:T(8,128)(2,1)S(1)} %bitcast.23, f32[128,128]{1,0:T(8,128)S(1)} %bitcast.25), custom_call_target="tpu_custom_call" | custom-call | tf_op jit(solution)/shard_map/coupling/pallas_call | solution.py:219
  43.4 1.0 %fold.2 = (bf16[2,128,128]{2,1,0:T(8,128)(2,1)S(1)}, f32[2,128,128]{2,1,0:T(8,128)S(1)}) custom-call(bf16[2,128,128]{2,1,0:T(8,128)(2,1)S(1)} %copy-done.5, bf16[2,128,128]{2,1,0:T(8,128)(2,1)} %collective-permute-done.9.refs_1_, bf16[2,128,128]{2,1,0:T(8,128)(2,1)} %collective-permute-done.10.refs_2_, bf16[2,128,128]{2,1,0:T(8,128)(2,1)} %collective-permute-done.11.refs_3_, ...), custom_call_target="tpu_custom_call" | custom-call | tf_op jit(solution)/shard_map/fold/pallas_call | solution.py:253
  44.4 3.1 %collective-permute-start.13 = (bf16[2,128,128]{2,1,0:T(8,128)(2,1)S(1)}, bf16[2,128,128]{2,1,0:T(8,128)(2,1)S(1)}, u32[]{:S(2)}, u32[]{:S(2)}) collective-permute-start(bf16[2,128,128]{2,1,0:T(8,128)(2,1)S(1)} %get-tuple-element.55), channel_id=1, source_target_pairs={{0,4},{1,5},{2,6},{3,7},{4,0},{5,1},{6,2},{7,3},{8,12},{9,13},{10,... | collective-permute-start | bytes 196616 | tf_op jit(solution)/shard_map/ppermute | solution.py:29
  47.6 3.9 %collective-permute-done.13.refs_1_ = bf16[2,128,128]{2,1,0:T(8,128)(2,1)S(1)} collective-permute-done((bf16[2,128,128]{2,1,0:T(8,128)(2,1)S(1)}, bf16[2,128,128]{2,1,0:T(8,128)(2,1)S(1)}, u32[]{:S(2)}, u32[]{:S(2)}) %collective-permute-start.13) | collective-permute-done | bytes 65568 | tf_op jit(solution)/shard_map/ppermute | solution.py:29
  51.5 0.9 %collective-permute-start.14 = (bf16[2,128,128]{2,1,0:T(8,128)(2,1)S(1)}, bf16[2,128,128]{2,1,0:T(8,128)(2,1)S(1)}, u32[]{:S(2)}, u32[]{:S(2)}) collective-permute-start(bf16[2,128,128]{2,1,0:T(8,128)(2,1)S(1)} %finish.2.refs_0_.refs_2_), channel_id=1, source_target_pairs={{0,1},{1,0},{2,3},{3,2},{4,5},{5,4},{6,7},{7,6},{8,9},{9,8},{10,11... | collective-permute-start | bytes 196616 | tf_op jit(solution)/shard_map/ppermute | solution.py:29
  53.1 1.9 %collective-permute-start.16 = (bf16[2,128,128]{2,1,0:T(8,128)(2,1)S(1)}, bf16[2,128,128]{2,1,0:T(8,128)(2,1)S(1)}, u32[]{:S(2)}, u32[]{:S(2)}) collective-permute-start(bf16[2,128,128]{2,1,0:T(8,128)(2,1)S(1)} %finish.2.refs_0_.refs_2_), channel_id=1, source_target_pairs={{0,3},{1,2},{2,1},{3,0},{4,7},{5,6},{6,5},{7,4},{8,11},{9,10},{10,... | collective-permute-start | bytes 196616 | tf_op jit(solution)/shard_map/ppermute | solution.py:29
  56.7 1.6 %collective-permute-done.16.refs_3_.refs_5_ = bf16[2,128,128]{2,1,0:T(8,128)(2,1)S(1)} collective-permute-done((bf16[2,128,128]{2,1,0:T(8,128)(2,1)S(1)}, bf16[2,128,128]{2,1,0:T(8,128)(2,1)S(1)}, u32[]{:S(2)}, u32[]{:S(2)}) %collective-permute-start.16) | collective-permute-done | bytes 65568 | tf_op jit(solution)/shard_map/ppermute | solution.py:29
  58.3 1.3 %collective-permute-start.20 = (bf16[8,128,128]{2,1,0:T(8,128)(2,1)S(1)}, bf16[8,128,128]{2,1,0:T(8,128)(2,1)S(1)}, u32[]{:S(2)}, u32[]{:S(2)}) collective-permute-start(bf16[8,128,128]{2,1,0:T(8,128)(2,1)S(1)} %stack.3.own_ref), channel_id=1, source_target_pairs={{8,0},{16,8},{24,16},{9,1},{17,9},{25,17},{10,2},{18,10},{26,18},{... | collective-permute-start | bytes 786440 | tf_op jit(solution)/shard_map/ppermute | solution.py:56
  59.6 3.5 %ladder.3 = (bf16[2,128,128]{2,1,0:T(8,128)(2,1)S(1)}, bf16[2,128,128]{2,1,0:T(8,128)(2,1)S(1)}, bf16[2,128,128]{2,1,0:T(8,128)(2,1)S(1)}, bf16[2,128,128]{2,1,0:T(8,128)(2,1)S(1)}) custom-call(s32[3]{0:T(128)S(1)} %get-tuple-element.68.refs_0_, s32[3]{0:T(128)S(1)} %get-tuple-element.67.refs_1_, bf16[2,128,128]{2,1,0:T(8,128)(2,1)S(1)} %finish.2.refs_0_.refs_2_, ...), custom_call_target="tpu_custom_call" | custom-call | bytes 12582912 | tf_op jit(solution)/shard_map/ladder/pallas_call | solution.py:180
  63.1 0.9 %collective-permute-start.17 = (bf16[2,128,128]{2,1,0:T(8,128)(2,1)S(1)}, bf16[2,128,128]{2,1,0:T(8,128)(2,1)S(1)}, u32[]{:S(2)}, u32[]{:S(2)}) collective-permute-start(bf16[2,128,128]{2,1,0:T(8,128)(2,1)S(1)} %get-tuple-element.61), channel_id=1, source_target_pairs={{0,1},{1,0},{2,3},{3,2},{4,5},{5,4},{6,7},{7,6},{8,9},{9,8},{10,11... | collective-permute-start | bytes 196616 | tf_op jit(solution)/shard_map/ppermute | solution.py:29
  64.0 1.7 %collective-permute-start.18 = (bf16[2,128,128]{2,1,0:T(8,128)(2,1)S(1)}, bf16[2,128,128]{2,1,0:T(8,128)(2,1)S(1)}, u32[]{:S(2)}, u32[]{:S(2)}) collective-permute-start(bf16[2,128,128]{2,1,0:T(8,128)(2,1)S(1)} %get-tuple-element.62), channel_id=1, source_target_pairs={{0,2},{1,3},{2,0},{3,1},{4,6},{5,7},{6,4},{7,5},{8,10},{9,11},{10,... | collective-permute-start | bytes 196616 | tf_op jit(solution)/shard_map/ppermute | solution.py:29
  65.7 1.0 %collective-permute-start.19 = (bf16[2,128,128]{2,1,0:T(8,128)(2,1)S(1)}, bf16[2,128,128]{2,1,0:T(8,128)(2,1)S(1)}, u32[]{:S(2)}, u32[]{:S(2)}) collective-permute-start(bf16[2,128,128]{2,1,0:T(8,128)(2,1)S(1)} %get-tuple-element.63), channel_id=1, source_target_pairs={{0,3},{1,2},{2,1},{3,0},{4,7},{5,6},{6,5},{7,4},{8,11},{9,10},{10,... | collective-permute-start | bytes 196616 | tf_op jit(solution)/shard_map/ppermute | solution.py:29
  66.7 1.0 %coupling.3.refs_4_ = f32[128,128]{1,0:T(8,128)S(1)} custom-call(s32[4]{0:T(128)S(1)} %copy-done.7, bf16[8,128,128]{2,1,0:T(8,128)(2,1)S(1)} %stack.3.own_ref, bf16[8,128,128]{2,1,0:T(8,128)(2,1)S(1)} %collective-permute-done.20.next_ref, bf16[4,128,128]{2,1,0:T(8,128)(2,1)S(1)} %bitcast.24, f32[128,128]{1,0:T(8,128)S(1)} %bitcast.26), custom_call_target="tpu_custom_call" | custom-call | tf_op jit(solution)/shard_map/coupling/pallas_call | solution.py:219
  68.8 2.3 %collective-permute-done.19.refs_3_ = bf16[2,128,128]{2,1,0:T(8,128)(2,1)S(1)} collective-permute-done((bf16[2,128,128]{2,1,0:T(8,128)(2,1)S(1)}, bf16[2,128,128]{2,1,0:T(8,128)(2,1)S(1)}, u32[]{:S(2)}, u32[]{:S(2)}) %collective-permute-start.19) | collective-permute-done | bytes 65568 | tf_op jit(solution)/shard_map/ppermute | solution.py:29
  71.2 3.2 %collective-permute-start.21 = (bf16[1,128,128]{2,1,0:T(8,128)(2,1)S(1)}, bf16[1,128,128]{2,1,0:T(8,128)(2,1)S(1)}, u32[]{:S(2)}, u32[]{:S(2)}) collective-permute-start(bf16[1,128,128]{2,1,0:T(8,128)(2,1)S(1)} %get-tuple-element.66), channel_id=1, source_target_pairs={{0,4},{1,5},{2,6},{3,7},{4,0},{5,1},{6,2},{7,3},{8,12},{9,13},{10,... | collective-permute-start | bytes 98312 | tf_op jit(solution)/shard_map/ppermute | solution.py:29
  74.4 1.9 %collective-permute-done.21.refs_1_ = bf16[1,128,128]{2,1,0:T(8,128)(2,1)S(1)} collective-permute-done((bf16[1,128,128]{2,1,0:T(8,128)(2,1)S(1)}, bf16[1,128,128]{2,1,0:T(8,128)(2,1)S(1)}, u32[]{:S(2)}, u32[]{:S(2)}) %collective-permute-start.21) | collective-permute-done | bytes 32800 | tf_op jit(solution)/shard_map/ppermute | solution.py:29
  (56 shorter events, 11.4 us)
Async XLA Ops:
  0.0 12.0 %collective-permute-start = (bf16[1,128,128]{2,1,0:T(8,128)(2,1)}, bf16[1,128,128]{2,1,0:T(8,128)(2,1)S(1)}, u32[]{:S(2)}, u32[]{:S(2)}) collective-permute-start(bf16[1,128,128]{2,1,0:T(8,128)(2,1)} %param.9), channel_id=1, source_target_pairs={{0,4},{1,5},{2,6},{3,7},{4,0},{5,1},{6,2},{7,3},{8,12},{9,13},{10,... | collective-permute-start | bytes 98312 | tf_op jit(solution)/shard_map/ppermute | solution.py:29
  5.3 6.6 %collective-permute-start.1 = (f32[1,128]{1,0:T(1,128)S(1)}, f32[1,128]{1,0:T(1,128)S(1)}, u32[]{:S(2)}, u32[]{:S(2)}) collective-permute-start(f32[1,128]{1,0:T(1,128)S(1)} %broadcast_add_fusion.refs_6_.refs_3_), channel_id=1, source_target_pairs={{0,4},{1,5},{2,6},{3,7},{4,0},{5,1},{6,2},{7,3},{8,12},{9,13},{10,... | collective-permute-start | bytes 1544 | tf_op jit(solution)/shard_map/ppermute | solution.py:29
  5.4 5.7 %collective-permute-start.2 = (bf16[1,256,128]{2,1,0:T(8,128)(2,1)}, bf16[1,256,128]{2,1,0:T(8,128)(2,1)S(1)}, u32[]{:S(2)}, u32[]{:S(2)}) collective-permute-start(bf16[1,256,128]{2,1,0:T(8,128)(2,1)} %param.10), channel_id=1, source_target_pairs={{0,4},{1,5},{2,6},{3,7},{4,0},{5,1},{6,2},{7,3},{8,12},{9,13},{10,... | collective-permute-start | bytes 196616 | tf_op jit(solution)/shard_map/ppermute | solution.py:29
  12.0 7.5 %collective-permute-start.6 = (bf16[2,256,128]{2,1,0:T(8,128)(2,1)S(1)}, bf16[2,256,128]{2,1,0:T(8,128)(2,1)S(1)}, u32[]{:S(2)}, u32[]{:S(2)}) collective-permute-start(bf16[2,256,128]{2,1,0:T(8,128)(2,1)S(1)} %pad_maximum_fusion.refs_1_), channel_id=1, source_target_pairs={{0,1},{1,0},{2,3},{3,2},{4,5},{5,4},{6,7},{7,6},{8,9},{9,8},{10,11... | collective-permute-start | bytes 393224 | tf_op jit(solution)/shard_map/ppermute | solution.py:29
  13.6 8.1 %collective-permute-start.7 = (bf16[2,256,128]{2,1,0:T(8,128)(2,1)S(1)}, bf16[2,256,128]{2,1,0:T(8,128)(2,1)S(1)}, u32[]{:S(2)}, u32[]{:S(2)}) collective-permute-start(bf16[2,256,128]{2,1,0:T(8,128)(2,1)S(1)} %pad_maximum_fusion.refs_1_), channel_id=1, source_target_pairs={{0,2},{1,3},{2,0},{3,1},{4,6},{5,7},{6,4},{7,5},{8,10},{9,11},{10,... | collective-permute-start | bytes 393224 | tf_op jit(solution)/shard_map/ppermute | solution.py:29
  15.1 7.0 %collective-permute-start.8 = (bf16[2,256,128]{2,1,0:T(8,128)(2,1)S(1)}, bf16[2,256,128]{2,1,0:T(8,128)(2,1)S(1)}, u32[]{:S(2)}, u32[]{:S(2)}) collective-permute-start(bf16[2,256,128]{2,1,0:T(8,128)(2,1)S(1)} %pad_maximum_fusion.refs_1_), channel_id=1, source_target_pairs={{0,3},{1,2},{2,1},{3,0},{4,7},{5,6},{6,5},{7,4},{8,11},{9,10},{10,... | collective-permute-start | bytes 393224 | tf_op jit(solution)/shard_map/ppermute | solution.py:29
  16.3 11.9 %collective-permute-start.3 = (bf16[2,128,128]{2,1,0:T(8,128)(2,1)S(1)}, bf16[2,128,128]{2,1,0:T(8,128)(2,1)S(1)}, u32[]{:S(2)}, u32[]{:S(2)}) collective-permute-start(bf16[2,128,128]{2,1,0:T(8,128)(2,1)S(1)} %constant_dynamic-update-slice_fusion.refs_0_.refs_2_), channel_id=1, source_target_pairs={{0,1},{1,0},{2,3},{3,2},{4,5},{5,4},{6,7},{7,6},{8,9},{9,8},{10,11... | collective-permute-start | bytes 196616 | tf_op jit(solution)/shard_map/ppermute | solution.py:29
  17.9 10.3 %collective-permute-start.4 = (bf16[2,128,128]{2,1,0:T(8,128)(2,1)S(1)}, bf16[2,128,128]{2,1,0:T(8,128)(2,1)S(1)}, u32[]{:S(2)}, u32[]{:S(2)}) collective-permute-start(bf16[2,128,128]{2,1,0:T(8,128)(2,1)S(1)} %constant_dynamic-update-slice_fusion.refs_0_.refs_2_), channel_id=1, source_target_pairs={{0,2},{1,3},{2,0},{3,1},{4,6},{5,7},{6,4},{7,5},{8,10},{9,11},{10,... | collective-permute-start | bytes 196616 | tf_op jit(solution)/shard_map/ppermute | solution.py:29
  19.4 8.8 %collective-permute-start.5 = (bf16[2,128,128]{2,1,0:T(8,128)(2,1)S(1)}, bf16[2,128,128]{2,1,0:T(8,128)(2,1)S(1)}, u32[]{:S(2)}, u32[]{:S(2)}) collective-permute-start(bf16[2,128,128]{2,1,0:T(8,128)(2,1)S(1)} %constant_dynamic-update-slice_fusion.refs_0_.refs_2_), channel_id=1, source_target_pairs={{0,3},{1,2},{2,1},{3,0},{4,7},{5,6},{6,5},{7,4},{8,11},{9,10},{10,... | collective-permute-start | bytes 196616 | tf_op jit(solution)/shard_map/ppermute | solution.py:29
  22.1 7.5 %copy-start.8 = (f32[1,128]{1,0:T(1,128)S(1)}, f32[1,128]{1,0:T(1,128)}, u32[]{:S(2)}) copy-start(f32[1,128]{1,0:T(1,128)} %param.14) | copy-start | bytes 1540
  22.1 15.7 %copy-start.9 = (s32[1,4]{1,0:T(1,128)S(1)}, s32[1,4]{1,0:T(1,128)}, u32[]{:S(2)}) copy-start(s32[1,4]{1,0:T(1,128)} %param.17) | copy-start | bytes 52
  28.3 10.4 %collective-permute-start.12 = (bf16[8,128,128]{2,1,0:T(8,128)(2,1)S(1)}, bf16[8,128,128]{2,1,0:T(8,128)(2,1)}, u32[]{:S(2)}, u32[]{:S(2)}) collective-permute-start(bf16[8,128,128]{2,1,0:T(8,128)(2,1)S(1)} %stack.2.own_ref), channel_id=1, source_target_pairs={{8,0},{16,8},{24,16},{9,1},{17,9},{25,17},{10,2},{18,10},{26,18},{... | collective-permute-start | bytes 786440 | tf_op jit(solution)/shard_map/ppermute | solution.py:56
  33.7 0.6 copy-start.4
  34.3 8.2 %collective-permute-start.9 = (bf16[2,128,128]{2,1,0:T(8,128)(2,1)}, bf16[2,128,128]{2,1,0:T(8,128)(2,1)}, u32[]{:S(2)}, u32[]{:S(2)}) collective-permute-start(bf16[2,128,128]{2,1,0:T(8,128)(2,1)} %get-tuple-element.49), channel_id=1, source_target_pairs={{0,1},{1,0},{2,3},{3,2},{4,5},{5,4},{6,7},{7,6},{8,9},{9,8},{10,11... | collective-permute-start | bytes 196616 | tf_op jit(solution)/shard_map/ppermute | solution.py:29
  35.2 7.4 %collective-permute-start.10 = (bf16[2,128,128]{2,1,0:T(8,128)(2,1)}, bf16[2,128,128]{2,1,0:T(8,128)(2,1)}, u32[]{:S(2)}, u32[]{:S(2)}) collective-permute-start(bf16[2,128,128]{2,1,0:T(8,128)(2,1)} %get-tuple-element.50), channel_id=1, source_target_pairs={{0,2},{1,3},{2,0},{3,1},{4,6},{5,7},{6,4},{7,5},{8,10},{9,11},{10,... | collective-permute-start | bytes 196616 | tf_op jit(solution)/shard_map/ppermute | solution.py:29
  36.7 5.9 %collective-permute-start.11 = (bf16[2,128,128]{2,1,0:T(8,128)(2,1)}, bf16[2,128,128]{2,1,0:T(8,128)(2,1)}, u32[]{:S(2)}, u32[]{:S(2)}) collective-permute-start(bf16[2,128,128]{2,1,0:T(8,128)(2,1)} %get-tuple-element.51), channel_id=1, source_target_pairs={{0,3},{1,2},{2,1},{3,0},{4,7},{5,6},{6,5},{7,4},{8,11},{9,10},{10,... | collective-permute-start | bytes 196616 | tf_op jit(solution)/shard_map/ppermute | solution.py:29
  38.6 28.0 %copy-start.7 = (s32[4]{0:T(128)S(1)}, s32[4]{0:T(128)}, u32[]{:S(2)}) copy-start(s32[4]{0:T(128)} %bitcast_select_fusion.near) | copy-start | bytes 52
  38.7 0.9 %copy-start = (bf16[1,4,128,128]{3,2,1,0:T(8,128)(2,1)S(1)}, bf16[1,4,128,128]{3,2,1,0:T(8,128)(2,1)}, u32[]{:S(2)}) copy-start(bf16[1,4,128,128]{3,2,1,0:T(8,128)(2,1)} %param.12) | copy-start | bytes 393220
  39.6 0.8 %copy-start.2 = (f32[1,128,128]{2,1,0:T(8,128)S(1)}, f32[1,128,128]{2,1,0:T(8,128)}, u32[]{:S(2)}) copy-start(f32[1,128,128]{2,1,0:T(8,128)} %param.13) | copy-start | bytes 196612
  40.4 0.7 copy-start.6
  41.1 25.6 %copy-start.1 = (bf16[1,4,128,128]{3,2,1,0:T(8,128)(2,1)S(1)}, bf16[1,4,128,128]{3,2,1,0:T(8,128)(2,1)}, u32[]{:S(2)}) copy-start(bf16[1,4,128,128]{3,2,1,0:T(8,128)(2,1)} %param.12) | copy-start | bytes 393220
  41.1 25.6 %copy-start.3 = (f32[1,128,128]{2,1,0:T(8,128)S(1)}, f32[1,128,128]{2,1,0:T(8,128)}, u32[]{:S(2)}) copy-start(f32[1,128,128]{2,1,0:T(8,128)} %param.13) | copy-start | bytes 196612
  42.6 0.8 %copy-start.5 = (bf16[2,128,128]{2,1,0:T(8,128)(2,1)S(1)}, bf16[2,128,128]{2,1,0:T(8,128)(2,1)}, u32[]{:S(2)}) copy-start(bf16[2,128,128]{2,1,0:T(8,128)(2,1)} %copy-done.4) | copy-start | bytes 196612
  44.4 7.0 %collective-permute-start.13 = (bf16[2,128,128]{2,1,0:T(8,128)(2,1)S(1)}, bf16[2,128,128]{2,1,0:T(8,128)(2,1)S(1)}, u32[]{:S(2)}, u32[]{:S(2)}) collective-permute-start(bf16[2,128,128]{2,1,0:T(8,128)(2,1)S(1)} %get-tuple-element.55), channel_id=1, source_target_pairs={{0,4},{1,5},{2,6},{3,7},{4,0},{5,1},{6,2},{7,3},{8,12},{9,13},{10,... | collective-permute-start | bytes 196616 | tf_op jit(solution)/shard_map/ppermute | solution.py:29
  51.5 4.3 %collective-permute-start.14 = (bf16[2,128,128]{2,1,0:T(8,128)(2,1)S(1)}, bf16[2,128,128]{2,1,0:T(8,128)(2,1)S(1)}, u32[]{:S(2)}, u32[]{:S(2)}) collective-permute-start(bf16[2,128,128]{2,1,0:T(8,128)(2,1)S(1)} %finish.2.refs_0_.refs_2_), channel_id=1, source_target_pairs={{0,1},{1,0},{2,3},{3,2},{4,5},{5,4},{6,7},{7,6},{8,9},{9,8},{10,11... | collective-permute-start | bytes 196616 | tf_op jit(solution)/shard_map/ppermute | solution.py:29
  52.4 4.3 %collective-permute-start.15 = (bf16[2,128,128]{2,1,0:T(8,128)(2,1)S(1)}, bf16[2,128,128]{2,1,0:T(8,128)(2,1)S(1)}, u32[]{:S(2)}, u32[]{:S(2)}) collective-permute-start(bf16[2,128,128]{2,1,0:T(8,128)(2,1)S(1)} %finish.2.refs_0_.refs_2_), channel_id=1, source_target_pairs={{0,2},{1,3},{2,0},{3,1},{4,6},{5,7},{6,4},{7,5},{8,10},{9,11},{10,... | collective-permute-start | bytes 196616 | tf_op jit(solution)/shard_map/ppermute | solution.py:29
  53.1 5.2 %collective-permute-start.16 = (bf16[2,128,128]{2,1,0:T(8,128)(2,1)S(1)}, bf16[2,128,128]{2,1,0:T(8,128)(2,1)S(1)}, u32[]{:S(2)}, u32[]{:S(2)}) collective-permute-start(bf16[2,128,128]{2,1,0:T(8,128)(2,1)S(1)} %finish.2.refs_0_.refs_2_), channel_id=1, source_target_pairs={{0,3},{1,2},{2,1},{3,0},{4,7},{5,6},{6,5},{7,4},{8,11},{9,10},{10,... | collective-permute-start | bytes 196616 | tf_op jit(solution)/shard_map/ppermute | solution.py:29
  58.3 8.3 %collective-permute-start.20 = (bf16[8,128,128]{2,1,0:T(8,128)(2,1)S(1)}, bf16[8,128,128]{2,1,0:T(8,128)(2,1)S(1)}, u32[]{:S(2)}, u32[]{:S(2)}) collective-permute-start(bf16[8,128,128]{2,1,0:T(8,128)(2,1)S(1)} %stack.3.own_ref), channel_id=1, source_target_pairs={{8,0},{16,8},{24,16},{9,1},{17,9},{25,17},{10,2},{18,10},{26,18},{... | collective-permute-start | bytes 786440 | tf_op jit(solution)/shard_map/ppermute | solution.py:56
  63.1 4.9 %collective-permute-start.17 = (bf16[2,128,128]{2,1,0:T(8,128)(2,1)S(1)}, bf16[2,128,128]{2,1,0:T(8,128)(2,1)S(1)}, u32[]{:S(2)}, u32[]{:S(2)}) collective-permute-start(bf16[2,128,128]{2,1,0:T(8,128)(2,1)S(1)} %get-tuple-element.61), channel_id=1, source_target_pairs={{0,1},{1,0},{2,3},{3,2},{4,5},{5,4},{6,7},{7,6},{8,9},{9,8},{10,11... | collective-permute-start | bytes 196616 | tf_op jit(solution)/shard_map/ppermute | solution.py:29
  64.0 4.8 %collective-permute-start.18 = (bf16[2,128,128]{2,1,0:T(8,128)(2,1)S(1)}, bf16[2,128,128]{2,1,0:T(8,128)(2,1)S(1)}, u32[]{:S(2)}, u32[]{:S(2)}) collective-permute-start(bf16[2,128,128]{2,1,0:T(8,128)(2,1)S(1)} %get-tuple-element.62), channel_id=1, source_target_pairs={{0,2},{1,3},{2,0},{3,1},{4,6},{5,7},{6,4},{7,5},{8,10},{9,11},{10,... | collective-permute-start | bytes 196616 | tf_op jit(solution)/shard_map/ppermute | solution.py:29
  65.7 5.5 %collective-permute-start.19 = (bf16[2,128,128]{2,1,0:T(8,128)(2,1)S(1)}, bf16[2,128,128]{2,1,0:T(8,128)(2,1)S(1)}, u32[]{:S(2)}, u32[]{:S(2)}) collective-permute-start(bf16[2,128,128]{2,1,0:T(8,128)(2,1)S(1)} %get-tuple-element.63), channel_id=1, source_target_pairs={{0,3},{1,2},{2,1},{3,0},{4,7},{5,6},{6,5},{7,4},{8,11},{9,10},{10,... | collective-permute-start | bytes 196616 | tf_op jit(solution)/shard_map/ppermute | solution.py:29
  71.2 5.1 %collective-permute-start.21 = (bf16[1,128,128]{2,1,0:T(8,128)(2,1)S(1)}, bf16[1,128,128]{2,1,0:T(8,128)(2,1)S(1)}, u32[]{:S(2)}, u32[]{:S(2)}) collective-permute-start(bf16[1,128,128]{2,1,0:T(8,128)(2,1)S(1)} %get-tuple-element.66), channel_id=1, source_target_pairs={{0,4},{1,5},{2,6},{3,7},{4,0},{5,1},{6,2},{7,3},{8,12},{9,13},{10,... | collective-permute-start | bytes 98312 | tf_op jit(solution)/shard_map/ppermute | solution.py:29
where the time goes:
time: 77.6 us; the launch traced here: 77 us
  starting transfers between devices  35.4 us (46%)
  Pallas kernels  18.1 us (23%)
  waiting for transfers between devices  14.8 us (19%)
  local copies, waits for them, and re-layouts  4.87 us (6%)
  other arithmetic  3.06 us (4%)
  between operations  0.87 us (1%)
    ppermute x20, starting transfers between devices, exchange(): return lax.ppermute(value, axis, [(d, d ^ offset) for d in range(count)])  32.8 us
    ppermute x20, waiting for transfers between devices, exchange(): return lax.ppermute(value, axis, [(d, d ^ offset) for d in range(count)])  14.7 us
    pallas_call x2, Pallas kernels, ladder(): pl.pallas_call(kernel, grid=(CAP,), in_specs=[smem_spec()] * 2 + [vmem_sp...  7.59 us
    pallas_call x1, Pallas kernels, project(): pl.pallas_call(kernel, grid=(aux // step,), in_specs=[smem_spec()] + [pl....  6.1 us
    unnamed x21, local copies, waits for them, and re-layouts  4.64 us
    ppermute x2, starting transfers between devices, from_next(): return lax.ppermute(value, axis, [(d, d - 1) for d in range(1, count)])  2.58 us
    pallas_call x2, Pallas kernels, coupling(): pl.pallas_call(coupling_kernel, in_specs=[smem_spec()] + [pl.BlockSpec()]...  2.49 us
  transfers between devices with their start and end apart: 22, of which 10 were waited for; matrix products, arithmetic and copies ran while one was open for 5% of the time, Pallas kernels for 21%

commit v1 on v0

--- a/solution.py
+++ b/solution.py
@@ -201,13 +201,12 @@
 
 def coupling_kernel(near, own_ref, next_ref, inter_ref, ints_ref, out_ref):
     count = own_ref.shape[0]
-    total = ints_ref[...]
-    for n in range(inter_ref.shape[0]):
-        at = near[n]
-        own = own_ref[jnp.minimum(at, count - 1)]
-        far = next_ref[jnp.maximum(at - count, 0)]
-        amp = jnp.where(at < count, own, far)
-        inter = inter_ref[n]
+    total = ints_ref[0]
+    for n in range(inter_ref.shape[1]):
+        at = near[0, n]
+        place = place_of(lax.rem(at, count), "dev")
+        amp = jnp.where(at < count, own_ref[place], next_ref[place])
+        inter = inter_ref[0, n]
         mixed = jnp.dot(inter, amp, preferred_element_type=F32).astype(BF16)
         total = total + lax.dot_general(
             mixed, inter, CONTRACT_LAST, preferred_element_type=F32
@@ -220,8 +219,11 @@
         coupling_kernel,
         in_specs=[smem_spec()] + [pl.BlockSpec()] * 4,
         out_specs=vmem_spec(),
-        out_shape=jax.ShapeDtypeStruct(ints.shape, F32),
+        out_shape=jax.ShapeDtypeStruct(ints.shape[1:], F32),
         compiler_params=params(16),
+        cost_estimate=pl.CostEstimate(
+            flops=4 * inter.shape[1] * inter.shape[2] ** 3, bytes_accessed=0, transcendentals=0
+        ),
         name="coupling",
     )(near, own, following, inter, ints)
 
@@ -304,20 +306,13 @@
     chosen = listed[None, :] & (rank[None, :] == jnp.arange(CAP)[:, None])
     pairs = jnp.sum(jnp.where(chosen, places[None, :] + 1, 0), axis=1) - 1
     slots = jnp.where(pairs >= 0, place_of(pairs, "dev"), 0)
-    near = pair_next[0]
-    near = jnp.where(
-        near < count, place_of(near, "dev"), count + place_of(near - count, "dev")
-    )
-    inter = intersections[0]
-    ints = pair_integrals[0]
-
-    far_amps = exchange(amplitudes, "dev", opposite("dev"))
-    pair_bases = gather_across(bases, "dev")
+
     shifted = pno_energies + 0.5 * pair_shift[:, None]
     far_shifted = exchange(shifted, "dev", opposite("dev"))
-    amps, far_amps, far_shifted, pair_bases = lax.optimization_barrier(
-        (amplitudes, far_amps, far_shifted, pair_bases)
-    )
+    pair_bases = gather_across(bases, "dev")
+    amps, far_shifted = lax.optimization_barrier((amplitudes, far_shifted))
+    far_amps = exchange(amps, "dev", opposite("dev"))
+    amps, pair_bases = lax.optimization_barrier((amps, pair_bases))
     group_bases = gather_near(pair_bases, "dev")
     group_amps = gather_near(jnp.concatenate([amps, far_amps], axis=0), "dev")
     energies = (shifted.reshape(-1, 1), shifted, far_shifted.reshape(-1, 1), far_shifted)
@@ -329,7 +324,7 @@
         group_amps, stacked = lax.optimization_barrier((group_amps, stacked))
         following = from_next(stacked, "grp")
         terms = ladder(slots, pairs, group_amps, projected)
-        rest = coupling(near, stacked, following, inter, ints)
+        rest = coupling(pair_next, stacked, following, intersections, pair_integrals)
         send, keep = fold(last, exchange_near(terms, "dev"), rest, energies)
         update = finish(last, keep, exchange(send, "dev", opposite("dev")), *energies[:2])
         if not last:

time: 77.6 us -> 76.2 us (0.982)
  starting transfers between devices: 35.4 us -> 29.7 us
  waiting for transfers between devices: 14.8 us -> 19.1 us
    ppermute x20, starting transfers between devices: 32.8 us -> 27.1 us  [exchange(): return lax.ppermute(value, axis, [(d, d ^ offset) for d in range(count)])]
    ppermute x20, waiting for transfers between devices: 14.7 us -> 19.1 us  [exchange(): return lax.ppermute(value, axis, [(d, d ^ offset) for d in range(count)])]
    unnamed x21 -> x19, local copies, waits for them, and re-layouts: 4.64 us -> 5.27 us
  transfers between devices with their start and end apart: 22 -> 22, of which waited for: 10 -> 12; matrix products, arithmetic and copies ran while one was open for 5% -> 4% of each run, Pallas kernels for 21% -> 21%
where the time goes in v1:
time: 76.2 us; the launch traced here: 75.7 us
  starting transfers between devices  29.7 us (39%)
  waiting for transfers between devices  19.1 us (25%)
  Pallas kernels  18.1 us (24%)
  local copies, waits for them, and re-layouts  5.51 us (7%)
  other arithmetic  2.47 us (3%)
  between operations  0.82 us (1%)
    ppermute x20, starting transfers between devices, exchange(): return lax.ppermute(value, axis, [(d, d ^ offset) for d in range(count)])  27.1 us
    ppermute x20, waiting for transfers between devices, exchange(): return lax.ppermute(value, axis, [(d, d ^ offset) for d in range(count)])  19.1 us
    pallas_call x2, Pallas kernels, ladder(): pl.pallas_call(kernel, grid=(CAP,), in_specs=[smem_spec()] * 2 + [vmem_sp...  7.59 us
    pallas_call x1, Pallas kernels, project(): pl.pallas_call(kernel, grid=(aux // step,), in_specs=[smem_spec()] + [pl....  6.09 us
    unnamed x19, local copies, waits for them, and re-layouts  5.27 us
    ppermute x2, starting transfers between devices, from_next(): return lax.ppermute(value, axis, [(d, d - 1) for d in range(1, count)])  2.58 us
    pallas_call x2, Pallas kernels, coupling(): pl.pallas_call(coupling_kernel, in_specs=[smem_spec()] + [pl.BlockSpec()]...  2.49 us
  transfers between devices with their start and end apart: 22, of which 12 were waited for; matrix products, arithmetic and copies ran while one was open for 4% of the time, Pallas kernels for 21%

profile of v1, /device:TPU:0, one launch (start us, length us, event | category | flops | bytes accessed | tf_op | source)
XLA Modules:
  0.0 75.7 jit_solution(9705229810181242349)
XLA Ops:
  1.3 4.0 %collective-permute-start = (f32[1,128]{1,0:T(1,128)S(1)}, f32[1,128]{1,0:T(1,128)S(1)}, u32[]{:S(2)}, u32[]{:S(2)}) collective-permute-start(f32[1,128]{1,0:T(1,128)S(1)} %broadcast_add_fusion.refs_6_.refs_3_), channel_id=1, source_target_pairs={{0,4},{1,5},{2,6},{3,7},{4,0},{5,1},{6,2},{7,3},{8,12},{9,13},{10,... | collective-permute-start | bytes 1544 | tf_op jit(solution)/shard_map/ppermute | solution.py:29
  6.9 2.9 %collective-permute-start.2 = (bf16[1,128,128]{2,1,0:T(8,128)(2,1)}, bf16[1,128,128]{2,1,0:T(8,128)(2,1)S(1)}, u32[]{:S(2)}, u32[]{:S(2)}) collective-permute-start(bf16[1,128,128]{2,1,0:T(8,128)(2,1)} %param.9), channel_id=1, source_target_pairs={{0,4},{1,5},{2,6},{3,7},{4,0},{5,1},{6,2},{7,3},{8,12},{9,13},{10,... | collective-permute-start | bytes 98312 | tf_op jit(solution)/shard_map/ppermute | solution.py:29
  9.8 2.6 %collective-permute-done.1 = bf16[1,256,128]{2,1,0:T(8,128)(2,1)S(1)} collective-permute-done((bf16[1,256,128]{2,1,0:T(8,128)(2,1)}, bf16[1,256,128]{2,1,0:T(8,128)(2,1)S(1)}, u32[]{:S(2)}, u32[]{:S(2)}) %collective-permute-start.1) | collective-permute-done | bytes 65568 | tf_op jit(solution)/shard_map/ppermute | solution.py:29
  12.4 0.9 %pad_maximum_fusion.refs_1_ = bf16[2,256,128]{2,1,0:T(8,128)(2,1)S(1)} fusion(bf16[1,256,128]{2,1,0:T(8,128)(2,1)S(1)} %collective-permute-done.1, bf16[1,256,128]{2,1,0:T(8,128)(2,1)} %param.10), kind=kLoop, calls=%fused_computation | loop fusion | flops 65536 | bytes 262144 | tf_op jit(solution)/shard_map/concatenate | solution.py:37
  13.3 1.6 %collective-permute-start.6 = (bf16[2,256,128]{2,1,0:T(8,128)(2,1)S(1)}, bf16[2,256,128]{2,1,0:T(8,128)(2,1)S(1)}, u32[]{:S(2)}, u32[]{:S(2)}) collective-permute-start(bf16[2,256,128]{2,1,0:T(8,128)(2,1)S(1)} %pad_maximum_fusion.refs_1_), channel_id=1, source_target_pairs={{0,1},{1,0},{2,3},{3,2},{4,5},{5,4},{6,7},{7,6},{8,9},{9,8},{10,11... | collective-permute-start | bytes 393224 | tf_op jit(solution)/shard_map/ppermute | solution.py:29
  14.9 2.0 %collective-permute-start.8 = (bf16[2,256,128]{2,1,0:T(8,128)(2,1)S(1)}, bf16[2,256,128]{2,1,0:T(8,128)(2,1)S(1)}, u32[]{:S(2)}, u32[]{:S(2)}) collective-permute-start(bf16[2,256,128]{2,1,0:T(8,128)(2,1)S(1)} %pad_maximum_fusion.refs_1_), channel_id=1, source_target_pairs={{0,3},{1,2},{2,1},{3,0},{4,7},{5,6},{6,5},{7,4},{8,11},{9,10},{10,... | collective-permute-start | bytes 393224 | tf_op jit(solution)/shard_map/ppermute | solution.py:29
  17.6 1.6 %collective-permute-start.3 = (bf16[2,128,128]{2,1,0:T(8,128)(2,1)S(1)}, bf16[2,128,128]{2,1,0:T(8,128)(2,1)S(1)}, u32[]{:S(2)}, u32[]{:S(2)}) collective-permute-start(bf16[2,128,128]{2,1,0:T(8,128)(2,1)S(1)} %constant_dynamic-update-slice_fusion.refs_0_.refs_2_), channel_id=1, source_target_pairs={{0,1},{1,0},{2,3},{3,2},{4,5},{5,4},{6,7},{7,6},{8,9},{9,8},{10,11... | collective-permute-start | bytes 196616 | tf_op jit(solution)/shard_map/ppermute | solution.py:29
  19.6 1.6 %collective-permute-start.5 = (bf16[2,128,128]{2,1,0:T(8,128)(2,1)S(1)}, bf16[2,128,128]{2,1,0:T(8,128)(2,1)S(1)}, u32[]{:S(2)}, u32[]{:S(2)}) collective-permute-start(bf16[2,128,128]{2,1,0:T(8,128)(2,1)S(1)} %constant_dynamic-update-slice_fusion.refs_0_.refs_2_), channel_id=1, source_target_pairs={{0,3},{1,2},{2,1},{3,0},{4,7},{5,6},{6,5},{7,4},{8,11},{9,10},{10,... | collective-permute-start | bytes 196616 | tf_op jit(solution)/shard_map/ppermute | solution.py:29
  22.0 6.1 %project.1.refs_6_ = bf16[3,16,128,256]{3,2,1,0:T(8,128)(2,1)S(1)} custom-call(s32[3]{0:T(128)S(1)} %get-tuple-element.68.refs_0_, bf16[2,256,128]{2,1,0:T(8,128)(2,1)S(1)} %pad_maximum_fusion.refs_1_, bf16[2,256,128]{2,1,0:T(8,128)(2,1)S(1)} %collective-permute-done.6.refs_2_, bf16[2,256,128]{2,1,0:T(8,128)(2,1)S(1)} %collective-permute-done.7.refs_3_, ...), custom_call_target="tpu_custom_call" | custom-call | flops 2415919104 | bytes 4194304 | tf_op jit(solution)/shard_map/project/pallas_call | solution.py:112
  28.1 1.3 %collective-permute-start.12 = (bf16[8,128,128]{2,1,0:T(8,128)(2,1)S(1)}, bf16[8,128,128]{2,1,0:T(8,128)(2,1)}, u32[]{:S(2)}, u32[]{:S(2)}) collective-permute-start(bf16[8,128,128]{2,1,0:T(8,128)(2,1)S(1)} %stack.2.own_ref), channel_id=1, source_target_pairs={{8,0},{16,8},{24,16},{9,1},{17,9},{25,17},{10,2},{18,10},{26,18},{... | collective-permute-start | bytes 786440 | tf_op jit(solution)/shard_map/ppermute | solution.py:56
  29.4 4.1 %ladder.2 = (bf16[2,128,128]{2,1,0:T(8,128)(2,1)S(1)}, bf16[2,128,128]{2,1,0:T(8,128)(2,1)}, bf16[2,128,128]{2,1,0:T(8,128)(2,1)}, bf16[2,128,128]{2,1,0:T(8,128)(2,1)}) custom-call(s32[3]{0:T(128)S(1)} %get-tuple-element.68.refs_0_, s32[3]{0:T(128)S(1)} %get-tuple-element.67.refs_1_, ...), custom_call_target="tpu_custom_call" | custom-call | bytes 12582912 | tf_op jit(solution)/shard_map/ladder/pallas_call | solution.py:180
  34.2 1.5 %collective-permute-start.9 = (bf16[2,128,128]{2,1,0:T(8,128)(2,1)}, bf16[2,128,128]{2,1,0:T(8,128)(2,1)}, u32[]{:S(2)}, u32[]{:S(2)}) collective-permute-start(bf16[2,128,128]{2,1,0:T(8,128)(2,1)} %get-tuple-element.49), channel_id=1, source_target_pairs={{0,1},{1,0},{2,3},{3,2},{4,5},{5,4},{6,7},{7,6},{8,9},{9,8},{10,11... | collective-permute-start | bytes 196616 | tf_op jit(solution)/shard_map/ppermute | solution.py:29
  36.4 1.2 %collective-permute-start.11 = (bf16[2,128,128]{2,1,0:T(8,128)(2,1)}, bf16[2,128,128]{2,1,0:T(8,128)(2,1)}, u32[]{:S(2)}, u32[]{:S(2)}) collective-permute-start(bf16[2,128,128]{2,1,0:T(8,128)(2,1)} %get-tuple-element.51), channel_id=1, source_target_pairs={{0,3},{1,2},{2,1},{3,0},{4,7},{5,6},{6,5},{7,4},{8,11},{9,10},{10,... | collective-permute-start | bytes 196616 | tf_op jit(solution)/shard_map/ppermute | solution.py:29
  37.9 0.9 %copy-done = bf16[1,4,128,128]{3,2,1,0:T(8,128)(2,1)S(1)} copy-done((bf16[1,4,128,128]{3,2,1,0:T(8,128)(2,1)S(1)}, bf16[1,4,128,128]{3,2,1,0:T(8,128)(2,1)}, u32[]{:S(2)}) %copy-start) | copy-done | bytes 131096
  40.3 1.5 %coupling.2.refs_4_ = f32[128,128]{1,0:T(8,128)S(1)} custom-call(s32[1,4]{1,0:T(1,128)S(1)} %copy-done.6, bf16[8,128,128]{2,1,0:T(8,128)(2,1)S(1)} %stack.2.own_ref, bf16[8,128,128]{2,1,0:T(8,128)(2,1)} %collective-permute-done.12.next_ref, bf16[1,4,128,128]{3,2,1,0:T(8,128)(2,1)S(1)} %copy-done, f32[1,128,128]{2,1,0:T(8,128)S(1)} %copy-done.2), custom_call_target="tpu_custom_call" | custom-call | flops 33554432 | tf_op jit(solution)/shard_map/coupling/pallas_call | solution.py:218
  43.0 1.0 %fold.2 = (bf16[2,128,128]{2,1,0:T(8,128)(2,1)S(1)}, f32[2,128,128]{2,1,0:T(8,128)S(1)}) custom-call(bf16[2,128,128]{2,1,0:T(8,128)(2,1)S(1)} %copy-done.5, bf16[2,128,128]{2,1,0:T(8,128)(2,1)} %collective-permute-done.9.refs_1_, bf16[2,128,128]{2,1,0:T(8,128)(2,1)} %collective-permute-done.10.refs_2_, bf16[2,128,128]{2,1,0:T(8,128)(2,1)} %collective-permute-done.11.refs_3_, ...), custom_call_target="tpu_custom_call" | custom-call | tf_op jit(solution)/shard_map/fold/pallas_call | solution.py:255
  44.1 1.1 %collective-permute-start.13 = (bf16[2,128,128]{2,1,0:T(8,128)(2,1)S(1)}, bf16[2,128,128]{2,1,0:T(8,128)(2,1)S(1)}, u32[]{:S(2)}, u32[]{:S(2)}) collective-permute-start(bf16[2,128,128]{2,1,0:T(8,128)(2,1)S(1)} %get-tuple-element.55), channel_id=1, source_target_pairs={{0,4},{1,5},{2,6},{3,7},{4,0},{5,1},{6,2},{7,3},{8,12},{9,13},{10,... | collective-permute-start | bytes 196616 | tf_op jit(solution)/shard_map/ppermute | solution.py:29
  45.2 5.1 %collective-permute-done.13.refs_1_ = bf16[2,128,128]{2,1,0:T(8,128)(2,1)S(1)} collective-permute-done((bf16[2,128,128]{2,1,0:T(8,128)(2,1)S(1)}, bf16[2,128,128]{2,1,0:T(8,128)(2,1)S(1)}, u32[]{:S(2)}, u32[]{:S(2)}) %collective-permute-start.13) | collective-permute-done | bytes 65568 | tf_op jit(solution)/shard_map/ppermute | solution.py:29
  50.4 1.7 %collective-permute-start.14 = (bf16[2,128,128]{2,1,0:T(8,128)(2,1)S(1)}, bf16[2,128,128]{2,1,0:T(8,128)(2,1)S(1)}, u32[]{:S(2)}, u32[]{:S(2)}) collective-permute-start(bf16[2,128,128]{2,1,0:T(8,128)(2,1)S(1)} %finish.2.refs_0_.refs_2_), channel_id=1, source_target_pairs={{0,1},{1,0},{2,3},{3,2},{4,5},{5,4},{6,7},{7,6},{8,9},{9,8},{10,11... | collective-permute-start | bytes 196616 | tf_op jit(solution)/shard_map/ppermute | solution.py:29
  52.1 1.9 %collective-permute-start.16 = (bf16[2,128,128]{2,1,0:T(8,128)(2,1)S(1)}, bf16[2,128,128]{2,1,0:T(8,128)(2,1)S(1)}, u32[]{:S(2)}, u32[]{:S(2)}) collective-permute-start(bf16[2,128,128]{2,1,0:T(8,128)(2,1)S(1)} %finish.2.refs_0_.refs_2_), channel_id=1, source_target_pairs={{0,3},{1,2},{2,1},{3,0},{4,7},{5,6},{6,5},{7,4},{8,11},{9,10},{10,... | collective-permute-start | bytes 196616 | tf_op jit(solution)/shard_map/ppermute | solution.py:29
  54.7 1.6 %collective-permute-done.15.refs_2_.refs_4_ = bf16[2,128,128]{2,1,0:T(8,128)(2,1)S(1)} collective-permute-done((bf16[2,128,128]{2,1,0:T(8,128)(2,1)S(1)}, bf16[2,128,128]{2,1,0:T(8,128)(2,1)S(1)}, u32[]{:S(2)}, u32[]{:S(2)}) %collective-permute-start.15) | collective-permute-done | bytes 65568 | tf_op jit(solution)/shard_map/ppermute | solution.py:29
  56.3 0.9 %collective-permute-done.16.refs_3_.refs_5_ = bf16[2,128,128]{2,1,0:T(8,128)(2,1)S(1)} collective-permute-done((bf16[2,128,128]{2,1,0:T(8,128)(2,1)S(1)}, bf16[2,128,128]{2,1,0:T(8,128)(2,1)S(1)}, u32[]{:S(2)}, u32[]{:S(2)}) %collective-permute-start.16) | collective-permute-done | bytes 65568 | tf_op jit(solution)/shard_map/ppermute | solution.py:29
  57.3 1.3 %collective-permute-start.20 = (bf16[8,128,128]{2,1,0:T(8,128)(2,1)S(1)}, bf16[8,128,128]{2,1,0:T(8,128)(2,1)S(1)}, u32[]{:S(2)}, u32[]{:S(2)}) collective-permute-start(bf16[8,128,128]{2,1,0:T(8,128)(2,1)S(1)} %stack.3.own_ref), channel_id=1, source_target_pairs={{8,0},{16,8},{24,16},{9,1},{17,9},{25,17},{10,2},{18,10},{26,18},{... | collective-permute-start | bytes 786440 | tf_op jit(solution)/shard_map/ppermute | solution.py:56
  58.6 3.5 %ladder.3 = (bf16[2,128,128]{2,1,0:T(8,128)(2,1)S(1)}, bf16[2,128,128]{2,1,0:T(8,128)(2,1)S(1)}, bf16[2,128,128]{2,1,0:T(8,128)(2,1)S(1)}, bf16[2,128,128]{2,1,0:T(8,128)(2,1)S(1)}) custom-call(s32[3]{0:T(128)S(1)} %get-tuple-element.68.refs_0_, s32[3]{0:T(128)S(1)} %get-tuple-element.67.refs_1_, bf16[2,128,128]{2,1,0:T(8,128)(2,1)S(1)} %finish.2.refs_0_.refs_2_, ...), custom_call_target="tpu_custom_call" | custom-call | bytes 12582912 | tf_op jit(solution)/shard_map/ladder/pallas_call | solution.py:180
  62.0 1.3 %collective-permute-start.17 = (bf16[2,128,128]{2,1,0:T(8,128)(2,1)S(1)}, bf16[2,128,128]{2,1,0:T(8,128)(2,1)S(1)}, u32[]{:S(2)}, u32[]{:S(2)}) collective-permute-start(bf16[2,128,128]{2,1,0:T(8,128)(2,1)S(1)} %get-tuple-element.61), channel_id=1, source_target_pairs={{0,1},{1,0},{2,3},{3,2},{4,5},{5,4},{6,7},{7,6},{8,9},{9,8},{10,11... | collective-permute-start | bytes 196616 | tf_op jit(solution)/shard_map/ppermute | solution.py:29
  63.4 1.2 %collective-permute-start.18 = (bf16[2,128,128]{2,1,0:T(8,128)(2,1)S(1)}, bf16[2,128,128]{2,1,0:T(8,128)(2,1)S(1)}, u32[]{:S(2)}, u32[]{:S(2)}) collective-permute-start(bf16[2,128,128]{2,1,0:T(8,128)(2,1)S(1)} %get-tuple-element.62), channel_id=1, source_target_pairs={{0,2},{1,3},{2,0},{3,1},{4,6},{5,7},{6,4},{7,5},{8,10},{9,11},{10,... | collective-permute-start | bytes 196616 | tf_op jit(solution)/shard_map/ppermute | solution.py:29
  64.6 1.0 %collective-permute-start.19 = (bf16[2,128,128]{2,1,0:T(8,128)(2,1)S(1)}, bf16[2,128,128]{2,1,0:T(8,128)(2,1)S(1)}, u32[]{:S(2)}, u32[]{:S(2)}) collective-permute-start(bf16[2,128,128]{2,1,0:T(8,128)(2,1)S(1)} %get-tuple-element.63), channel_id=1, source_target_pairs={{0,3},{1,2},{2,1},{3,0},{4,7},{5,6},{6,5},{7,4},{8,11},{9,10},{10,... | collective-permute-start | bytes 196616 | tf_op jit(solution)/shard_map/ppermute | solution.py:29
  66.3 1.0 %coupling.3.refs_4_ = f32[128,128]{1,0:T(8,128)S(1)} custom-call(s32[1,4]{1,0:T(1,128)S(1)} %copy-done.7, bf16[8,128,128]{2,1,0:T(8,128)(2,1)S(1)} %stack.3.own_ref, bf16[8,128,128]{2,1,0:T(8,128)(2,1)S(1)} %collective-permute-done.20.next_ref, bf16[1,4,128,128]{3,2,1,0:T(8,128)(2,1)S(1)} %copy-done.1, f32[1,128,128]{2,1,0:T(8,128)S(1)} %copy-done.3), custom_call_target="tpu_custom_call" | custom-call | flops 33554432 | tf_op jit(solution)/shard_map/coupling/pallas_call | solution.py:218
  67.3 0.9 %collective-permute-done.18.refs_2_ = bf16[2,128,128]{2,1,0:T(8,128)(2,1)S(1)} collective-permute-done((bf16[2,128,128]{2,1,0:T(8,128)(2,1)S(1)}, bf16[2,128,128]{2,1,0:T(8,128)(2,1)S(1)}, u32[]{:S(2)}, u32[]{:S(2)}) %collective-permute-start.18) | collective-permute-done | bytes 65568 | tf_op jit(solution)/shard_map/ppermute | solution.py:29
  68.2 1.8 %collective-permute-done.19.refs_3_ = bf16[2,128,128]{2,1,0:T(8,128)(2,1)S(1)} collective-permute-done((bf16[2,128,128]{2,1,0:T(8,128)(2,1)S(1)}, bf16[2,128,128]{2,1,0:T(8,128)(2,1)S(1)}, u32[]{:S(2)}, u32[]{:S(2)}) %collective-permute-start.19) | collective-permute-done | bytes 65568 | tf_op jit(solution)/shard_map/ppermute | solution.py:29
  70.1 1.7 %collective-permute-start.21 = (bf16[1,128,128]{2,1,0:T(8,128)(2,1)S(1)}, bf16[1,128,128]{2,1,0:T(8,128)(2,1)S(1)}, u32[]{:S(2)}, u32[]{:S(2)}) collective-permute-start(bf16[1,128,128]{2,1,0:T(8,128)(2,1)S(1)} %get-tuple-element.66), channel_id=1, source_target_pairs={{0,4},{1,5},{2,6},{3,7},{4,0},{5,1},{6,2},{7,3},{8,12},{9,13},{10,... | collective-permute-start | bytes 98312 | tf_op jit(solution)/shard_map/ppermute | solution.py:29
  71.7 3.2 %collective-permute-done.21.refs_1_ = bf16[1,128,128]{2,1,0:T(8,128)(2,1)S(1)} collective-permute-done((bf16[1,128,128]{2,1,0:T(8,128)(2,1)S(1)}, bf16[1,128,128]{2,1,0:T(8,128)(2,1)S(1)}, u32[]{:S(2)}, u32[]{:S(2)}) %collective-permute-start.21) | collective-permute-done | bytes 32800 | tf_op jit(solution)/shard_map/ppermute | solution.py:29
  (53 shorter events, 10.7 us)
Async XLA Ops:
  1.3 5.6 %collective-permute-start = (f32[1,128]{1,0:T(1,128)S(1)}, f32[1,128]{1,0:T(1,128)S(1)}, u32[]{:S(2)}, u32[]{:S(2)}) collective-permute-start(f32[1,128]{1,0:T(1,128)S(1)} %broadcast_add_fusion.refs_6_.refs_3_), channel_id=1, source_target_pairs={{0,4},{1,5},{2,6},{3,7},{4,0},{5,1},{6,2},{7,3},{8,12},{9,13},{10,... | collective-permute-start | bytes 1544 | tf_op jit(solution)/shard_map/ppermute | solution.py:29
  5.3 7.1 %collective-permute-start.1 = (bf16[1,256,128]{2,1,0:T(8,128)(2,1)}, bf16[1,256,128]{2,1,0:T(8,128)(2,1)S(1)}, u32[]{:S(2)}, u32[]{:S(2)}) collective-permute-start(bf16[1,256,128]{2,1,0:T(8,128)(2,1)} %param.10), channel_id=1, source_target_pairs={{0,4},{1,5},{2,6},{3,7},{4,0},{5,1},{6,2},{7,3},{8,12},{9,13},{10,... | collective-permute-start | bytes 196616 | tf_op jit(solution)/shard_map/ppermute | solution.py:29
  6.9 10.7 %collective-permute-start.2 = (bf16[1,128,128]{2,1,0:T(8,128)(2,1)}, bf16[1,128,128]{2,1,0:T(8,128)(2,1)S(1)}, u32[]{:S(2)}, u32[]{:S(2)}) collective-permute-start(bf16[1,128,128]{2,1,0:T(8,128)(2,1)} %param.9), channel_id=1, source_target_pairs={{0,4},{1,5},{2,6},{3,7},{4,0},{5,1},{6,2},{7,3},{8,12},{9,13},{10,... | collective-permute-start | bytes 98312 | tf_op jit(solution)/shard_map/ppermute | solution.py:29
  13.3 6.4 %collective-permute-start.6 = (bf16[2,256,128]{2,1,0:T(8,128)(2,1)S(1)}, bf16[2,256,128]{2,1,0:T(8,128)(2,1)S(1)}, u32[]{:S(2)}, u32[]{:S(2)}) collective-permute-start(bf16[2,256,128]{2,1,0:T(8,128)(2,1)S(1)} %pad_maximum_fusion.refs_1_), channel_id=1, source_target_pairs={{0,1},{1,0},{2,3},{3,2},{4,5},{5,4},{6,7},{7,6},{8,9},{9,8},{10,11... | collective-permute-start | bytes 393224 | tf_op jit(solution)/shard_map/ppermute | solution.py:29
  14.9 6.4 %collective-permute-start.7 = (bf16[2,256,128]{2,1,0:T(8,128)(2,1)S(1)}, bf16[2,256,128]{2,1,0:T(8,128)(2,1)S(1)}, u32[]{:S(2)}, u32[]{:S(2)}) collective-permute-start(bf16[2,256,128]{2,1,0:T(8,128)(2,1)S(1)} %pad_maximum_fusion.refs_1_), channel_id=1, source_target_pairs={{0,2},{1,3},{2,0},{3,1},{4,6},{5,7},{6,4},{7,5},{8,10},{9,11},{10,... | collective-permute-start | bytes 393224 | tf_op jit(solution)/shard_map/ppermute | solution.py:29
  14.9 7.1 %collective-permute-start.8 = (bf16[2,256,128]{2,1,0:T(8,128)(2,1)S(1)}, bf16[2,256,128]{2,1,0:T(8,128)(2,1)S(1)}, u32[]{:S(2)}, u32[]{:S(2)}) collective-permute-start(bf16[2,256,128]{2,1,0:T(8,128)(2,1)S(1)} %pad_maximum_fusion.refs_1_), channel_id=1, source_target_pairs={{0,3},{1,2},{2,1},{3,0},{4,7},{5,6},{6,5},{7,4},{8,11},{9,10},{10,... | collective-permute-start | bytes 393224 | tf_op jit(solution)/shard_map/ppermute | solution.py:29
  17.6 10.4 %collective-permute-start.3 = (bf16[2,128,128]{2,1,0:T(8,128)(2,1)S(1)}, bf16[2,128,128]{2,1,0:T(8,128)(2,1)S(1)}, u32[]{:S(2)}, u32[]{:S(2)}) collective-permute-start(bf16[2,128,128]{2,1,0:T(8,128)(2,1)S(1)} %constant_dynamic-update-slice_fusion.refs_0_.refs_2_), channel_id=1, source_target_pairs={{0,1},{1,0},{2,3},{3,2},{4,5},{5,4},{6,7},{7,6},{8,9},{9,8},{10,11... | collective-permute-start | bytes 196616 | tf_op jit(solution)/shard_map/ppermute | solution.py:29
  19.2 8.9 %collective-permute-start.4 = (bf16[2,128,128]{2,1,0:T(8,128)(2,1)S(1)}, bf16[2,128,128]{2,1,0:T(8,128)(2,1)S(1)}, u32[]{:S(2)}, u32[]{:S(2)}) collective-permute-start(bf16[2,128,128]{2,1,0:T(8,128)(2,1)S(1)} %constant_dynamic-update-slice_fusion.refs_0_.refs_2_), channel_id=1, source_target_pairs={{0,2},{1,3},{2,0},{3,1},{4,6},{5,7},{6,4},{7,5},{8,10},{9,11},{10,... | collective-permute-start | bytes 196616 | tf_op jit(solution)/shard_map/ppermute | solution.py:29
  19.6 8.4 %collective-permute-start.5 = (bf16[2,128,128]{2,1,0:T(8,128)(2,1)S(1)}, bf16[2,128,128]{2,1,0:T(8,128)(2,1)S(1)}, u32[]{:S(2)}, u32[]{:S(2)}) collective-permute-start(bf16[2,128,128]{2,1,0:T(8,128)(2,1)S(1)} %constant_dynamic-update-slice_fusion.refs_0_.refs_2_), channel_id=1, source_target_pairs={{0,3},{1,2},{2,1},{3,0},{4,7},{5,6},{6,5},{7,4},{8,11},{9,10},{10,... | collective-permute-start | bytes 196616 | tf_op jit(solution)/shard_map/ppermute | solution.py:29
  22.0 15.7 %copy-start.8 = (f32[1,128]{1,0:T(1,128)S(1)}, f32[1,128]{1,0:T(1,128)}, u32[]{:S(2)}) copy-start(f32[1,128]{1,0:T(1,128)} %param.14) | copy-start | bytes 1540
  28.1 9.8 %collective-permute-start.12 = (bf16[8,128,128]{2,1,0:T(8,128)(2,1)S(1)}, bf16[8,128,128]{2,1,0:T(8,128)(2,1)}, u32[]{:S(2)}, u32[]{:S(2)}) collective-permute-start(bf16[8,128,128]{2,1,0:T(8,128)(2,1)S(1)} %stack.2.own_ref), channel_id=1, source_target_pairs={{8,0},{16,8},{24,16},{9,1},{17,9},{25,17},{10,2},{18,10},{26,18},{... | collective-permute-start | bytes 786440 | tf_op jit(solution)/shard_map/ppermute | solution.py:56
  33.5 0.6 copy-start.4
  34.2 7.6 %collective-permute-start.9 = (bf16[2,128,128]{2,1,0:T(8,128)(2,1)}, bf16[2,128,128]{2,1,0:T(8,128)(2,1)}, u32[]{:S(2)}, u32[]{:S(2)}) collective-permute-start(bf16[2,128,128]{2,1,0:T(8,128)(2,1)} %get-tuple-element.49), channel_id=1, source_target_pairs={{0,1},{1,0},{2,3},{3,2},{4,5},{5,4},{6,7},{7,6},{8,9},{9,8},{10,11... | collective-permute-start | bytes 196616 | tf_op jit(solution)/shard_map/ppermute | solution.py:29
  35.7 6.1 %collective-permute-start.10 = (bf16[2,128,128]{2,1,0:T(8,128)(2,1)}, bf16[2,128,128]{2,1,0:T(8,128)(2,1)}, u32[]{:S(2)}, u32[]{:S(2)}) collective-permute-start(bf16[2,128,128]{2,1,0:T(8,128)(2,1)} %get-tuple-element.50), channel_id=1, source_target_pairs={{0,2},{1,3},{2,0},{3,1},{4,6},{5,7},{6,4},{7,5},{8,10},{9,11},{10,... | collective-permute-start | bytes 196616 | tf_op jit(solution)/shard_map/ppermute | solution.py:29
  36.4 5.8 %collective-permute-start.11 = (bf16[2,128,128]{2,1,0:T(8,128)(2,1)}, bf16[2,128,128]{2,1,0:T(8,128)(2,1)}, u32[]{:S(2)}, u32[]{:S(2)}) collective-permute-start(bf16[2,128,128]{2,1,0:T(8,128)(2,1)} %get-tuple-element.51), channel_id=1, source_target_pairs={{0,3},{1,2},{2,1},{3,0},{4,7},{5,6},{6,5},{7,4},{8,11},{9,10},{10,... | collective-permute-start | bytes 196616 | tf_op jit(solution)/shard_map/ppermute | solution.py:29
  37.9 0.9 %copy-start = (bf16[1,4,128,128]{3,2,1,0:T(8,128)(2,1)S(1)}, bf16[1,4,128,128]{3,2,1,0:T(8,128)(2,1)}, u32[]{:S(2)}) copy-start(bf16[1,4,128,128]{3,2,1,0:T(8,128)(2,1)} %inter_ref.3) | copy-start | bytes 393220
  38.8 0.8 %copy-start.2 = (f32[1,128,128]{2,1,0:T(8,128)S(1)}, f32[1,128,128]{2,1,0:T(8,128)}, u32[]{:S(2)}) copy-start(f32[1,128,128]{2,1,0:T(8,128)} %ints_ref.3) | copy-start | bytes 196612
  39.6 0.7 copy-start.6
  40.3 25.3 %copy-start.1 = (bf16[1,4,128,128]{3,2,1,0:T(8,128)(2,1)S(1)}, bf16[1,4,128,128]{3,2,1,0:T(8,128)(2,1)}, u32[]{:S(2)}) copy-start(bf16[1,4,128,128]{3,2,1,0:T(8,128)(2,1)} %inter_ref.3) | copy-start | bytes 393220
  40.3 25.3 %copy-start.3 = (f32[1,128,128]{2,1,0:T(8,128)S(1)}, f32[1,128,128]{2,1,0:T(8,128)}, u32[]{:S(2)}) copy-start(f32[1,128,128]{2,1,0:T(8,128)} %ints_ref.3) | copy-start | bytes 196612
  42.2 0.8 %copy-start.5 = (bf16[2,128,128]{2,1,0:T(8,128)(2,1)S(1)}, bf16[2,128,128]{2,1,0:T(8,128)(2,1)}, u32[]{:S(2)}) copy-start(bf16[2,128,128]{2,1,0:T(8,128)(2,1)} %copy-done.4) | copy-start | bytes 196612
  44.1 6.3 %collective-permute-start.13 = (bf16[2,128,128]{2,1,0:T(8,128)(2,1)S(1)}, bf16[2,128,128]{2,1,0:T(8,128)(2,1)S(1)}, u32[]{:S(2)}, u32[]{:S(2)}) collective-permute-start(bf16[2,128,128]{2,1,0:T(8,128)(2,1)S(1)} %get-tuple-element.55), channel_id=1, source_target_pairs={{0,4},{1,5},{2,6},{3,7},{4,0},{5,1},{6,2},{7,3},{8,12},{9,13},{10,... | collective-permute-start | bytes 196616 | tf_op jit(solution)/shard_map/ppermute | solution.py:29
  50.4 4.3 %collective-permute-start.14 = (bf16[2,128,128]{2,1,0:T(8,128)(2,1)S(1)}, bf16[2,128,128]{2,1,0:T(8,128)(2,1)S(1)}, u32[]{:S(2)}, u32[]{:S(2)}) collective-permute-start(bf16[2,128,128]{2,1,0:T(8,128)(2,1)S(1)} %finish.2.refs_0_.refs_2_), channel_id=1, source_target_pairs={{0,1},{1,0},{2,3},{3,2},{4,5},{5,4},{6,7},{7,6},{8,9},{9,8},{10,11... | collective-permute-start | bytes 196616 | tf_op jit(solution)/shard_map/ppermute | solution.py:29
  52.1 4.3 %collective-permute-start.15 = (bf16[2,128,128]{2,1,0:T(8,128)(2,1)S(1)}, bf16[2,128,128]{2,1,0:T(8,128)(2,1)S(1)}, u32[]{:S(2)}, u32[]{:S(2)}) collective-permute-start(bf16[2,128,128]{2,1,0:T(8,128)(2,1)S(1)} %finish.2.refs_0_.refs_2_), channel_id=1, source_target_pairs={{0,2},{1,3},{2,0},{3,1},{4,6},{5,7},{6,4},{7,5},{8,10},{9,11},{10,... | collective-permute-start | bytes 196616 | tf_op jit(solution)/shard_map/ppermute | solution.py:29
  52.1 5.2 %collective-permute-start.16 = (bf16[2,128,128]{2,1,0:T(8,128)(2,1)S(1)}, bf16[2,128,128]{2,1,0:T(8,128)(2,1)S(1)}, u32[]{:S(2)}, u32[]{:S(2)}) collective-permute-start(bf16[2,128,128]{2,1,0:T(8,128)(2,1)S(1)} %finish.2.refs_0_.refs_2_), channel_id=1, source_target_pairs={{0,3},{1,2},{2,1},{3,0},{4,7},{5,6},{6,5},{7,4},{8,11},{9,10},{10,... | collective-permute-start | bytes 196616 | tf_op jit(solution)/shard_map/ppermute | solution.py:29
  57.3 8.3 %collective-permute-start.20 = (bf16[8,128,128]{2,1,0:T(8,128)(2,1)S(1)}, bf16[8,128,128]{2,1,0:T(8,128)(2,1)S(1)}, u32[]{:S(2)}, u32[]{:S(2)}) collective-permute-start(bf16[8,128,128]{2,1,0:T(8,128)(2,1)S(1)} %stack.3.own_ref), channel_id=1, source_target_pairs={{8,0},{16,8},{24,16},{9,1},{17,9},{25,17},{10,2},{18,10},{26,18},{... | collective-permute-start | bytes 786440 | tf_op jit(solution)/shard_map/ppermute | solution.py:56
  62.0 5.3 %collective-permute-start.17 = (bf16[2,128,128]{2,1,0:T(8,128)(2,1)S(1)}, bf16[2,128,128]{2,1,0:T(8,128)(2,1)S(1)}, u32[]{:S(2)}, u32[]{:S(2)}) collective-permute-start(bf16[2,128,128]{2,1,0:T(8,128)(2,1)S(1)} %get-tuple-element.61), channel_id=1, source_target_pairs={{0,1},{1,0},{2,3},{3,2},{4,5},{5,4},{6,7},{7,6},{8,9},{9,8},{10,11... | collective-permute-start | bytes 196616 | tf_op jit(solution)/shard_map/ppermute | solution.py:29
  63.4 4.8 %collective-permute-start.18 = (bf16[2,128,128]{2,1,0:T(8,128)(2,1)S(1)}, bf16[2,128,128]{2,1,0:T(8,128)(2,1)S(1)}, u32[]{:S(2)}, u32[]{:S(2)}) collective-permute-start(bf16[2,128,128]{2,1,0:T(8,128)(2,1)S(1)} %get-tuple-element.62), channel_id=1, source_target_pairs={{0,2},{1,3},{2,0},{3,1},{4,6},{5,7},{6,4},{7,5},{8,10},{9,11},{10,... | collective-permute-start | bytes 196616 | tf_op jit(solution)/shard_map/ppermute | solution.py:29
  64.6 5.5 %collective-permute-start.19 = (bf16[2,128,128]{2,1,0:T(8,128)(2,1)S(1)}, bf16[2,128,128]{2,1,0:T(8,128)(2,1)S(1)}, u32[]{:S(2)}, u32[]{:S(2)}) collective-permute-start(bf16[2,128,128]{2,1,0:T(8,128)(2,1)S(1)} %get-tuple-element.63), channel_id=1, source_target_pairs={{0,3},{1,2},{2,1},{3,0},{4,7},{5,6},{6,5},{7,4},{8,11},{9,10},{10,... | collective-permute-start | bytes 196616 | tf_op jit(solution)/shard_map/ppermute | solution.py:29
  65.6 0.7 copy-start.7
  70.1 4.9 %collective-permute-start.21 = (bf16[1,128,128]{2,1,0:T(8,128)(2,1)S(1)}, bf16[1,128,128]{2,1,0:T(8,128)(2,1)S(1)}, u32[]{:S(2)}, u32[]{:S(2)}) collective-permute-start(bf16[1,128,128]{2,1,0:T(8,128)(2,1)S(1)} %get-tuple-element.66), channel_id=1, source_target_pairs={{0,4},{1,5},{2,6},{3,7},{4,0},{5,1},{6,2},{7,3},{8,12},{9,13},{10,... | collective-permute-start | bytes 98312 | tf_op jit(solution)/shard_map/ppermute | solution.py:29
